TPU v7x, 32 devices: a whole 2x2x4 slice. The times are simulated.
32 devices in a mesh: groups: 2 (over x), wide: 16 (over z, y, core).
Axes of the slice: x: 2, y: 2, z: 4, core: 2. Of those that a mesh axis runs over, the one named last changes fastest.
Arguments:
- loader_features: bfloat16 [32768, 128], P(('groups', 'wide')), parts along dimension 0, may hold values from -6 to 6
- dest: int32 [32768], P(('groups', 'wide')), parts along dimension 0, may hold values from 0 to 16383, as said below
- block_values: bfloat16 [8192, 128, 128], P(('groups', 'wide')), parts along dimension 0, may hold values from -0.09375 to 0.09375
- row_block: int32 [8192], P(('groups', 'wide')), parts along dimension 0, may hold values from 0 to 7, as said below
- col_block: int32 [8192], P(('groups', 'wide')), parts along dimension 0, may hold values from 0 to 127, as said below
- w_first: bfloat16 [128, 256], replicated, may hold values from -0.5 to 0.5
- b_first: float32 [256], replicated, may hold values from -3 to 3
- w_second: bfloat16 [256, 256], replicated, may hold values from -0.375 to 0.375
- b_second: float32 [256], replicated, may hold values from -3 to 3
Outputs:
- output: bfloat16 [32768, 256], P(('groups', 'wide')), parts along dimension 0
There are 2 independent parts, one for each index of `groups`. A program takes and returns all parts, laid end to end along the dimension named above; an argument that names none is the same for every part. Nothing has to cross between parts.
Inputs may be any that keep to these rules, and one draw needn't show every extreme that they name: dest is a permutation; row i goes to owner dest[i] // 1024. Each device sends at most 256 of its rows to one owner and exactly 256 to some owner; every owner receives exactly 256 rows from some device. `col_block`: A device's list holds 16 groups of 16 entries; in group g every column block lies in device g's nodes (g * 8 to g * 8 + 7); the k-th entry's column block depends only on k mod 2, and these 2 are distinct. `row_block`: in each group, the k-th entry's row block is distinct among entries with the same k mod 2.
All inputs are finite; a program needn't handle non-finite values.
Results may differ from a plain program's by a relative error of at most 0.0058.
Values may be sent and summed in bfloat16 or wider, within the bound.
A program may use at most 128 MiB of HBM per device.

v0:
```python
import math

import jax
import jax.numpy as jnp
from jax import lax
from jax.sharding import PartitionSpec as P


def body(
    loader_features, dest, block_values, row_block, col_block, w_first, b_first, w_second, b_second
):
    devices = lax.axis_size("wide")
    own_index = lax.axis_index("wide")
    node_dev = loader_features.shape[0]
    feature_width = loader_features.shape[1]
    block_size = block_values.shape[1]
    row_blocks = node_dev // block_size
    slots = block_values.shape[0] // devices
    used = slots // row_blocks
    batch_groups = math.gcd(devices, 8)
    all_rows = lax.all_gather(loader_features, "wide", axis=0, tiled=True)
    all_dest = lax.all_gather(dest, "wide", axis=0, tiled=True)
    local = all_dest - own_index * node_dev
    local = jnp.where((local >= 0) & (local < node_dev), local, node_dev)
    features = (
        jnp.zeros((node_dev + 1, feature_width), jnp.bfloat16).at[local].set(all_rows)[:node_dev]
    )
    grid_rows = row_block.reshape(devices, row_blocks, used)
    order = jnp.argsort(grid_rows, axis=1, stable=True)
    grid_values = block_values.reshape(devices, row_blocks, used, block_size, block_size)
    ordered = jnp.take_along_axis(grid_values, order[:, :, :, None, None], axis=1)
    group_cols = col_block.reshape(devices, row_blocks, used)[:, 0, :]

    def aggregate(panel):
        width = panel.shape[1]
        empty = jnp.zeros((row_blocks, block_size, width), jnp.float32)
        carry = empty
        piece = lax.all_gather(panel, "wide", axis=0, tiled=True)
        start = jnp.int32(0)
        length = piece.shape[0]
        tile_count = length // block_size
        piece_tiles = piece.reshape(tile_count, block_size, width)
        first_group = start // node_dev
        covered = -(-length // node_dev) + 0
        covered = min(devices, covered)
        span = min(covered, batch_groups)
        for batch in range(-(-covered // span)):
            wanted_group = first_group + batch * span
            begin = jnp.minimum(wanted_group, devices - span)
            values = lax.dynamic_slice_in_dim(ordered, begin, span, 0)
            cols = lax.dynamic_slice_in_dim(group_cols, begin, span, 0)
            group_of = begin + jnp.arange(span, dtype=jnp.int32)
            valid = (cols >= 0) & (cols < tile_count) & (group_of[:, None] >= wanted_group)
            picked = jnp.take(piece_tiles, jnp.clip(cols, 0, tile_count - 1), axis=0)
            picked = picked * valid.astype(jnp.bfloat16)[:, :, None, None]
            carry = carry + jnp.einsum(
                "gruij,gujw->riw", values, picked, preferred_element_type=jnp.float32
            )
        return carry.reshape(node_dev, width)

    first = aggregate(features).astype(jnp.bfloat16)
    hidden = jax.nn.relu(
        jnp.dot(first, w_first, preferred_element_type=jnp.float32) + b_first
    ).astype(jnp.bfloat16)
    second = aggregate(hidden).astype(jnp.bfloat16)
    output = jnp.dot(second, w_second, preferred_element_type=jnp.float32) + b_second
    return output.astype(jnp.bfloat16)


def solution(mesh):
    placed = (
        P(("groups", "wide"), None),
        P(("groups", "wide")),
        P(("groups", "wide"), None, None),
        P(("groups", "wide")),
        P(("groups", "wide")),
        P(),
        P(),
        P(),
        P(),
    )
    return jax.shard_map(
        body, mesh=mesh, in_specs=placed, out_specs=P(("groups", "wide"), None), check_vma=False
    )
```

profile of v0, /device:TPU:0, one launch (start us, length us, event | category | flops | bytes accessed | tf_op | source)
XLA Modules:
  0.0 262.6 jit_solution(10796248333810704136)
XLA Ops:
  6.5 0.0 copy-start
  6.5 0.0 all-gather.4.cloned.1.call-start
  6.5 0.7 all-gather.4.cloned.1.call-update
  7.3 0.0 all-gather.6.cloned.1.call-start
  7.3 23.6 %all_gather.12 = s32[16384]{0:T(1024)S(1)} all-gather(s32[1024]{0:T(1024)} %param.14), channel_id=1, replica_groups=mesh['groups'=2,'wide'=16] {'wide'}, dimensions={0}, use_global_device_ids=true | all-gather | bytes 69632 | tf_op jit(solution)/shard_map/all_gather | solution.py:22
  31.0 31.9 %all-gather.4.cloned.1.call-done = bf16[16384,128]{1,0:T(8,128)(2,1)} async-done(((bf16[1024,128]{1,0:T(8,128)(2,1)}), bf16[16384,128]{1,0:T(8,128)(2,1)}) %all-gather.4.cloned.1.call-update) | async-done | bytes 4194320 | tf_op jit(solution)/shard_map/all_gather | solution.py:21
  62.9 41.4 %scatter_custom_fusion = bf16[1025,128]{1,0:T(8,128)(2,1)S(1)} fusion(s32[16384]{0:T(1024)S(1)} %compare_select_fusion, bf16[16384,128]{1,0:T(8,128)(2,1)} %all-gather.4.cloned.1.call-done, bf16[]{:T(256)} %constant.78.clone.1), kind=kCustom, calls=%fused_computation.50 | custom fusion | bytes 262912 | tf_op jit(solution)/shard_map/scatter | solution.py:26
  104.3 0.7 slice.22
  105.0 0.0 all-gather.6.cloned.1.call-update
  105.1 0.0 all-gather.8.cloned.1.call-start
  105.1 0.8 reshape.122
  105.9 0.8 reshape.126
  106.8 0.1 copy.79
  106.8 0.1 copy.78
  106.9 0.1 copy.57
  107.1 0.1 copy.62
  107.2 0.1 copy.60
  107.3 0.1 copy.64
  107.4 0.1 copy.59
  107.4 0.1 reshape.189
  107.5 0.1 copy.63
  107.6 0.1 reshape.193
  107.7 5.3 %sort.17 = (s32[16,8,2]{2,1,0:T(8,128)}, s32[16,8,2]{2,1,0:T(8,128)S(1)}) sort(s32[16,8,2]{2,1,0:T(8,128)S(1)} %reshape.122, s32[16,8,2]{2,1,0:T(8,128)S(1)} %iota.16), dimensions={1}, to_apply=%region_0.1 | sort | flops 2048 | bytes 4096 | tf_op jit(solution)/shard_map/jit(argsort)/sort | solution.py:29
  113.0 0.1 reshape.161
  113.1 14.2 %gather_fusion = bf16[256,128,128]{2,1,0:T(8,128)(2,1)} fusion(bf16[16,8,2,128,128]{4,3,2,1,0:T(8,128)(2,1)} %bitcast.79, s32[256]{0:T(256)S(1)} %reshape.161), kind=kCustom, calls=%fused_computation.4 | custom fusion | bytes 16780288 | tf_op jit(solution)/shard_map/jit(take_along_axis)/gather | solution.py:31
  127.4 27.0 %all-gather.6.cloned.1.call-done = bf16[16384,128]{1,0:T(8,128)(2,1)} async-done(((bf16[1024,128]{1,0:T(8,128)(2,1)}), bf16[16384,128]{1,0:T(8,128)(2,1)}) %all-gather.6.cloned.1.call-update) | async-done | bytes 4194320 | tf_op jit(solution)/shard_map/all_gather | solution.py:38
  154.4 2.8 %gather_fusion.1 = bf16[16,128,128]{2,1,0:T(8,128)(2,1)S(1)} fusion(bf16[128,128,128]{2,1,0:T(8,128)(2,1)} %bitcast.93, s32[1024]{0:T(1024)S(1)} %pad_clamp_fusion.1), kind=kCustom, calls=%fused_computation.clone | custom fusion | bytes 1048640 | tf_op jit(solution)/shard_map/jit(_take)/gather | solution.py:54
  157.3 2.8 %gather_fusion.2 = bf16[16,128,128]{2,1,0:T(8,128)(2,1)S(1)} fusion(bf16[128,128,128]{2,1,0:T(8,128)(2,1)} %bitcast.94, s32[1024]{0:T(1024)S(1)} %pad_clamp_fusion), kind=kCustom, calls=%fused_computation.2.clone | custom fusion | bytes 1048640 | tf_op jit(solution)/shard_map/jit(_take)/gather | solution.py:54
  160.1 0.0 copy-start.1
  160.1 0.0 copy-start.2
  160.1 0.0 copy-start.3
  160.1 3.7 %fusion.15 = f32[8,128,128]{2,1,0:T(8,128)S(1)} fusion(bf16[16,8,2,128,128]{4,3,2,1,0:T(8,128)(2,1)} %bitcast.80, pred[16,8,2]{2,1,0:T(8,128)(4,1)S(1)} %compare_and_fusion, bf16[8,2,128,128]{3,2,1,0:T(8,128)(2,1)S(1)} %bitcast.91, pred[8,2]{1,0:T(8,128)(4,1)S(1)} %copy.57, bf16[8,2]{1,0:T(8,128)(2,1)S(1)} %copy.60), kind=kOutput, calls=%fused_computation.24 | convolution fusion | flops 542375936 | bytes 9437488 | tf_op jit(solution)/shard_map/gruij,gujw->riw/dot_general | solution.py:56
  163.8 0.9 copy-done.1
  164.8 1.4 fusion.18
  166.1 0.0 copy-done.2
  166.1 0.0 copy-done.3
  166.2 1.1 fusion.13
  167.2 0.0 all-gather.8.cloned.1.call-update
  167.3 73.5 %all-gather.8.cloned.1.call-done = bf16[16384,256]{1,0:T(8,128)(2,1)} async-done(((bf16[1024,256]{1,0:T(8,128)(2,1)}), bf16[16384,256]{1,0:T(8,128)(2,1)}) %all-gather.8.cloned.1.call-update) | async-done | bytes 8388624 | tf_op jit(solution)/shard_map/all_gather | solution.py:38
  240.8 4.0 %gather_fusion.4 = bf16[16,128,256]{2,1,0:T(8,128)(2,1)S(1)} fusion(bf16[128,128,256]{2,1,0:T(8,128)(2,1)} %bitcast.88, s32[1024]{0:T(1024)S(1)} %pad_clamp_fusion), kind=kCustom, calls=%fused_computation.3.clone | custom fusion | bytes 2097216 | tf_op jit(solution)/shard_map/jit(_take)/gather | solution.py:54
  244.8 4.0 %gather_fusion.3 = bf16[16,128,256]{2,1,0:T(8,128)(2,1)S(1)} fusion(bf16[128,128,256]{2,1,0:T(8,128)(2,1)} %bitcast.89, s32[1024]{0:T(1024)S(1)} %pad_clamp_fusion.1), kind=kCustom, calls=%fused_computation.1.clone | custom fusion | bytes 2097216 | tf_op jit(solution)/shard_map/jit(_take)/gather | solution.py:54
  248.8 0.0 slice-start
  248.8 0.0 slice-start.1
  248.8 3.7 %fusion.8 = f32[8,128,256]{2,1,0:T(8,128)S(1)} fusion(bf16[16,8,2,128,128]{4,3,2,1,0:T(8,128)(2,1)} %bitcast.81, pred[16,8,2]{2,1,0:T(8,128)(4,1)S(1)} %compare_and_fusion, bf16[8,2,128,256]{3,2,1,0:T(8,128)(2,1)S(1)} %bitcast.87, pred[8,2]{1,0:T(8,128)(4,1)S(1)} %copy.57, bf16[8,2]{1,0:T(8,128)(2,1)S(1)} %copy.60), kind=kOutput, calls=%fused_computation.15 | convolution fusion | flops 1080557568 | bytes 10486064 | tf_op jit(solution)/shard_map/gruij,gujw->riw/dot_general | solution.py:56
  252.6 0.0 slice-done
  252.6 1.0 slice-done.1
  253.5 0.0 copy-start.4
  253.5 1.4 fusion.12
  255.0 0.0 copy-done
  255.0 0.0 copy-done.4
  255.0 1.1 fusion.14
  (14 shorter events, 0.1 us)
Async XLA Ops:
  6.5 248.4 %copy-start = (bf16[256,256]{1,0:T(8,128)(2,1)S(1)}, bf16[256,256]{1,0:T(8,128)(2,1)}, u32[]{:S(2)}) copy-start(bf16[256,256]{1,0:T(8,128)(2,1)} %param.20) | copy-start | bytes 393220
  6.5 56.4 %all-gather.4.cloned.1.call-start = ((), (), s32[]{:S(2)}) async-start(), calls=%async_computation | async-start | bytes 4456448 | tf_op jit(solution)/shard_map/all_gather | solution.py:21
  7.3 147.2 %all-gather.6.cloned.1.call-start = ((), (), s32[]{:S(2)}) async-start(), calls=%async_computation.1 | async-start | bytes 4456448 | tf_op jit(solution)/shard_map/all_gather | solution.py:38
  105.1 135.8 %all-gather.8.cloned.1.call-start = ((), (), s32[]{:S(2)}) async-start(), calls=%async_computation.2 | async-start | bytes 8912896 | tf_op jit(solution)/shard_map/all_gather | solution.py:38
  160.1 4.6 %copy-start.1 = (bf16[256,128,128]{2,1,0:T(8,128)(2,1)S(1)}, bf16[256,128,128]{2,1,0:T(8,128)(2,1)}, u32[]{:S(2)}) copy-start(bf16[256,128,128]{2,1,0:T(8,128)(2,1)} %gather_fusion) | copy-start | bytes 25165828
  160.1 6.0 %copy-start.2 = (bf16[128,256]{1,0:T(8,128)(2,1)S(1)}, bf16[128,256]{1,0:T(8,128)(2,1)}, u32[]{:S(2)}) copy-start(bf16[128,256]{1,0:T(8,128)(2,1)} %param.18) | copy-start | bytes 196612
  160.1 6.0 %copy-start.3 = (f32[256]{0:T(256)S(1)}, f32[256]{0:T(256)}, u32[]{:S(2)}) copy-start(f32[256]{0:T(256)} %param.19) | copy-start | bytes 3076
  248.8 3.8 %slice-start = ((s8[8388608]{0:T(1024)(128)(4,1)}), s8[4194304]{0:T(1024)(128)(4,1)S(1)}, s32[]{:S(2)}) async-start(s8[8388608]{0:T(1024)(128)(4,1)} %bitcast.83), calls=%async_computation.3 | async-start | bytes 8388608
  248.8 4.7 %slice-start.1 = ((s8[8388608]{0:T(1024)(128)(4,1)}), s8[4194304]{0:T(1024)(128)(4,1)S(1)}, s32[]{:S(2)}) async-start(s8[8388608]{0:T(1024)(128)(4,1)} %bitcast.83), calls=%async_computation.4 | async-start | bytes 8388608
  253.5 1.4 copy-start.4
Sparse Core Ops, SparseCore 0:
  9.5 53.3 all-gather.3
  105.2 49.2 all-gather.5
  167.4 73.3 all-gather.7
where the time goes:
time: 263 us
  waiting for transfers between devices  133 us (51%)
  local copies, waits for them, and re-layouts  74.5 us (28%)
  blocking collectives  23.6 us (9%)
  between operations  13.3 us (5%)
  matrix products  12.4 us (5%)
  other arithmetic  5.39 us (2%)
    all_gather x2, waiting for transfers between devices, aggregate(): piece = lax.all_gather(panel, 'wide', axis=0, tiled=True)  101 us
    scatter x1, local copies, waits for them, and re-layouts, body(): jnp.zeros((node_dev + 1, feature_width), jnp.bfloat16).at[local]  41.4 us
    all_gather x1, waiting for transfers between devices, body(): all_rows = lax.all_gather(loader_features, 'wide', axis=0, tiled=True)  31.9 us
    all_gather x1, blocking collectives, body(): all_dest = lax.all_gather(dest, 'wide', axis=0, tiled=True)  23.6 us
    gather x2, local copies, waits for them, and re-layouts, body(): jnp.take_along_axis(grid_values, order[:, :, :, None, None], axis=1)  14.3 us
    gather x4, local copies, waits for them, and re-layouts, aggregate(): picked = jnp.take(piece_tiles, jnp.clip(cols, 0, tile_count - 1), axis=0)  13.7 us
    dot_general x4, matrix products, aggregate(): jnp.einsum('gruij,gujw->riw', values, picked, preferred_element_type=jnp....  10.2 us
    sort x1, other arithmetic, body(): order = jnp.argsort(grid_rows, axis=1, stable=True)  5.26 us
  transfers between devices with their start and end apart: 3, of which 3 were waited for; matrix products, arithmetic and copies ran while one was open for 8% of the time, Pallas kernels for 0%

commit v1 on v0

v1 whole, which is shorter than its diff:
```python
import functools

import jax
import jax.numpy as jnp
from jax import lax
from jax.experimental import pallas as pl
from jax.experimental.pallas import tpu as pltpu
from jax.sharding import PartitionSpec as P

MESH = pl.DeviceIdType.MESH
F32 = jnp.float32
BF16 = jnp.bfloat16
I32 = jnp.int32


def greet_all(n):
    me = lax.axis_index("wide")
    barrier = pltpu.get_barrier_semaphore()

    def greet(step, _):
        pl.semaphore_signal(
            barrier, inc=1, device_id={"wide": (me + step) % n}, device_id_type=MESH
        )
        return _

    lax.fori_loop(1, n, greet, 0)
    pl.semaphore_wait(barrier, n - 1)


def gather(depth, side, buf, own_ref, sems, extra, process):
    line_send, side_send, pair_send, recv = sems
    me = lax.axis_index("wide")
    core = me % 2
    lane_y = (me // 2) % side
    lane_z = me // (2 * side)
    pair = me + 1 - 2 * core

    def slot_of(at_z, at_y, at_core):
        return (at_z * side + at_y) * 2 + at_core

    def copy(source_ref, slot, send, target):
        return pltpu.make_async_remote_copy(
            src_ref=source_ref,
            dst_ref=buf.at[slot],
            send_sem=send,
            recv_sem=recv.at[slot],
            device_id={"wide": target},
            device_id_type=MESH,
        )

    def arrived(slot):
        copy(buf.at[slot], slot, pair_send.at[0, 0], pair).wait_recv()

    def place(d):
        off = (d + 1) // 2
        at_z = lane_z + off * (1 - 2 * (d % 2))
        valid = (d >= 0) & (at_z >= 0) & (at_z < depth)
        return at_z, valid

    right = slot_of(lane_z + 1, lane_y, core)
    left = slot_of(lane_z - 1, lane_y, core)
    across = slot_of(lane_z, 1 - lane_y, core)
    steps = 2 * depth - 1
    buf[me] = own_ref[...]

    def line_copies(d, slot):
        source = buf.at[slot]
        return (
            (copy(source, slot, line_send.at[0, d], right),
             ((d == 0) | (d % 2 == 1)) & (lane_z < depth - 1)),
            (copy(source, slot, line_send.at[1, d], left),
             (d % 2 == 0) & (lane_z > 0)),
        )

    def step(d, _):
        at_z, valid = place(d)

        @pl.when(valid & (d < steps))
        def _line():
            slot = slot_of(at_z, lane_y, core)

            @pl.when(d > 0)
            def _wait():
                arrived(slot)

            for one, go in line_copies(d, slot):
                pl.when(go)(one.start)
            if side == 2:
                copy(buf.at[slot], slot, side_send.at[d], across).start()
            copy(buf.at[slot], slot, pair_send.at[0, d], pair).start()

        extra(d)

        back_z, back_valid = place(d - 2)
        if side == 2:

            @pl.when(back_valid & (d - 2 < steps))
            def _side():
                slot = slot_of(back_z, 1 - lane_y, core)
                arrived(slot)
                copy(buf.at[slot], slot, pair_send.at[1, d - 2], pair).start()

        def kind(k, _):
            lag = jnp.where(k == 0, 0, jnp.where(k == 3, 4, 2))
            from_side = k % 2
            from_pair = k // 2
            kz, kvalid = place(d - lag)
            ky = jnp.where(from_side == 1, side - 1 - lane_y, lane_y)
            kc = jnp.where(from_pair == 1, 1 - core, core)
            slot = slot_of(kz, ky, kc)

            @pl.when(kvalid & (d - lag < steps))
            def _process():
                @pl.when(from_pair == 1)
                def _wait():
                    arrived(slot)

                process(slot)

            return _

        if side == 2:
            lax.fori_loop(0, 4, kind, 0)
        else:
            lax.fori_loop(0, 2, lambda k, c: kind(2 * k, c), 0)
        return _

    lax.fori_loop(0, steps + 4, step, 0)

    def drain(d, _):
        at_z, valid = place(d)

        @pl.when(valid)
        def _drain():
            slot = slot_of(at_z, lane_y, core)
            for one, go in line_copies(d, slot):
                pl.when(go)(one.wait_send)
            if side == 2:
                copy(buf.at[slot], slot, side_send.at[d], across).wait_send()
                other = slot_of(at_z, 1 - lane_y, core)
                copy(buf.at[other], other, pair_send.at[1, d], pair).wait_send()
            copy(buf.at[slot], slot, pair_send.at[0, d], pair).wait_send()

        return _

    lax.fori_loop(0, steps, drain, 0)


def rows_kernel(
    depth, side, dest_ref, loader_ref, table, inverse_int,
    rows_buf, dest_buf, inverse, dest_send, dest_recv, *sems
):
    n = depth * side * 2
    node_dev = loader_ref.shape[0]
    block = dest_ref.shape[1]
    row_blocks = node_dev // block
    me = lax.axis_index("wide")
    greet_all(n)

    def dest_copy(step, source):
        return pltpu.make_async_remote_copy(
            src_ref=dest_ref,
            dst_ref=dest_buf.at[source],
            send_sem=dest_send.at[step],
            recv_sem=dest_recv.at[source],
            device_id={"wide": (me + step) % n},
            device_id_type=MESH,
        )

    def send_dest(step, _):
        dest_copy(step, me).start()
        return _

    lax.fori_loop(1, n, send_dest, 0)
    dest_buf[me] = dest_ref[...]
    inverse[...] = jnp.zeros_like(inverse)

    blocks = n * row_blocks
    sub_hi = lax.broadcasted_iota(I32, (blocks, block), 0)
    sub_lo = lax.broadcasted_iota(I32, (block, block), 0)
    lane_hi = lax.broadcasted_iota(I32, (blocks, block), 1).astype(F32)

    def invert(source):
        @pl.when(source != me)
        def _wait():
            dest_copy(1, source).wait_recv()

        positions = dest_buf[source]
        upper, lower, right = [], [], []
        for a in range(row_blocks):
            line = positions[a : a + 1, :]
            hit = sub_hi == line // block
            number = (source * row_blocks + a).astype(F32)
            upper.append(jnp.where(hit, number, 0.0).astype(BF16))
            lower.append(jnp.where(hit, lane_hi, 0.0).astype(BF16))
            right.append(jnp.where(sub_lo == line % block, 1.0, 0.0).astype(BF16))
        left = jnp.concatenate(
            [jnp.concatenate(upper, axis=1), jnp.concatenate(lower, axis=1)], axis=0
        )
        inverse[...] += lax.dot_general(
            left,
            jnp.concatenate(right, axis=1),
            (((1,), (1,)), ((), ())),
            preferred_element_type=F32,
        )

    def invert_two(d):
        def one(k, _):
            source = 2 * d + k
            pl.when(source < n)(lambda: invert(source))
            return _

        lax.fori_loop(0, 2, one, 0)

    def widen(slot):
        start = pl.multiple_of(slot * node_dev, node_dev)
        table[pl.ds(start, node_dev), :] = rows_buf[slot].astype(F32)

    gather(depth, side, rows_buf, loader_ref, sems, invert_two, widen)

    def drain_dest(step, _):
        dest_copy(step, me).wait_send()
        return _

    lax.fori_loop(1, n, drain_dest, 0)

    inverse_int[...] = (
        inverse[:blocks, :] * float(block) + inverse[blocks:, :]
    ).astype(I32)


def add(group, right, values, total, row_blocks):
    block = values.shape[1]
    for r in range(row_blocks):
        at = (group * row_blocks + r) * 2
        left = jnp.concatenate([values[at], values[at + 1]], axis=1)
        total[pl.ds(r * block, block), :] += jnp.dot(
            left, right, preferred_element_type=F32
        )


def first_kernel(
    n, col_ref, order_ref, inverse_ref, table_ref, values_ref, first_ref, ordered_ref,
    values, picked, total, local_sem
):
    def load_block(at, _):
        pltpu.make_async_copy(
            values_ref.at[order_ref[at]], values.at[at], local_sem.at[0]
        ).start()
        return _

    lax.fori_loop(0, values.shape[0], load_block, 0, unroll=8)
    block = values.shape[1]
    row_blocks = first_ref.shape[0] // block
    slots = values.shape[0] // n

    def pick(t, _):
        column = col_ref[(t // 2) * slots + t % 2]

        def fetch(j, _):
            for k in range(16):
                row = inverse_ref[column, j * 16 + k]
                picked[pl.ds(t * block + j * 16 + k, 1), :] = table_ref[pl.ds(row, 1), :]
            return _

        return lax.fori_loop(0, block // 16, fetch, _)

    lax.fori_loop(0, 2 * n, pick, 0)
    pltpu.make_async_copy(values_ref, values, local_sem.at[0]).wait()
    store = pltpu.make_async_copy(values, ordered_ref, local_sem.at[1])
    store.start()
    total[...] = jnp.zeros_like(total)

    def group_step(group, _):
        start = pl.multiple_of(group * 2 * block, 2 * block)
        right = picked[pl.ds(start, 2 * block), :].astype(BF16)
        add(group, right, values, total, row_blocks)
        return _

    lax.fori_loop(0, n, group_step, 0)
    first_ref[...] = total[...].astype(BF16)
    store.wait()


def second_kernel(
    depth, side, col_ref, first_ref, values_ref,
    w_first_ref, b_first_ref, w_second_ref, b_second_ref, out_ref,
    values, first_buf, total, local_sem, *sems
):
    n = depth * side * 2
    load = pltpu.make_async_copy(values_ref, values, local_sem)
    load.start()
    block = values.shape[1]
    row_blocks = first_ref.shape[0] // block
    slots = values.shape[0] // n
    greet_all(n)
    total[...] = jnp.zeros_like(total)
    load.wait()

    def second_group(slot):
        tiles = []
        for u in range(2):
            column = col_ref[slot * slots + u] - slot * row_blocks
            tile = first_buf[slot, :block]
            for b in range(1, row_blocks):
                tile = jnp.where(
                    column == b, first_buf[slot, b * block : (b + 1) * block], tile
                )
            tiles.append(tile)
        tiles = jnp.concatenate(tiles, axis=0)
        hidden = jnp.dot(tiles, w_first_ref[...], preferred_element_type=F32)
        hidden = jnp.maximum(hidden + b_first_ref[...], 0.0).astype(BF16)
        add(slot, hidden, values, total, row_blocks)

    gather(depth, side, first_buf, first_ref, sems, lambda d: None, second_group)
    out_ref[...] = (
        jnp.dot(total[...].astype(BF16), w_second_ref[...], preferred_element_type=F32)
        + b_second_ref[...]
    ).astype(BF16)


def body(
    depth, side,
    loader_features, dest, block_values, row_block, col_block, w_first, b_first, w_second, b_second
):
    n = depth * side * 2
    node_dev, width = loader_features.shape
    count, block, _ = block_values.shape
    row_blocks = node_dev // block
    slots = count // n
    used = slots // row_blocks
    hidden = w_first.shape[1]
    blocks = n * row_blocks
    grid_rows = row_block.reshape(n, row_blocks, 1, used)
    hit = grid_rows == jnp.arange(row_blocks, dtype=I32)[None, None, :, None]
    number = jnp.arange(count, dtype=I32).reshape(n, row_blocks, 1, used)
    order = jnp.sum(jnp.where(hit, number, 0), axis=1).reshape(count)
    steps = 2 * depth - 1
    vmem = pl.BlockSpec(memory_space=pltpu.VMEM)
    smem = pl.BlockSpec(memory_space=pltpu.SMEM)
    dma = pltpu.SemaphoreType.DMA
    anywhere = pl.BlockSpec(memory_space=pl.ANY)
    line_sems = [dma((2, steps)), dma((steps,)), dma((2, steps)), dma((n,))]

    def params(**more):
        return pltpu.CompilerParams(vmem_limit_bytes=60 * 1024 * 1024, **more)

    table, inverse = pl.pallas_call(
        functools.partial(rows_kernel, depth, side),
        out_shape=(
            jax.ShapeDtypeStruct((n * node_dev, width), F32),
            jax.ShapeDtypeStruct((blocks, block), I32),
        ),
        in_specs=[vmem] * 2,
        out_specs=(vmem, vmem),
        scratch_shapes=[
            pltpu.VMEM((n, node_dev, width), BF16),
            pltpu.VMEM((n, row_blocks, block), I32),
            pltpu.VMEM((2 * blocks, block), F32),
            dma((n,)),
            dma((n,)),
            *line_sems,
        ],
        compiler_params=params(collective_id=0, has_side_effects=True),
    )(dest.reshape(row_blocks, block), loader_features)
    first, ordered = pl.pallas_call(
        functools.partial(first_kernel, n),
        out_shape=(
            jax.ShapeDtypeStruct((node_dev, width), BF16),
            jax.ShapeDtypeStruct(block_values.shape, BF16),
        ),
        in_specs=[smem, smem, smem, vmem, anywhere],
        out_specs=(vmem, anywhere),
        scratch_shapes=[
            pltpu.VMEM((count, block, block), BF16),
            pltpu.VMEM((n * used * block, width), F32),
            pltpu.VMEM((node_dev, width), F32),
            dma((2,)),
        ],
        compiler_params=params(),
    )(col_block, order, inverse, table, block_values)
    return pl.pallas_call(
        functools.partial(second_kernel, depth, side),
        out_shape=jax.ShapeDtypeStruct((node_dev, w_second.shape[1]), BF16),
        in_specs=[smem, vmem, anywhere] + [vmem] * 4,
        out_specs=vmem,
        scratch_shapes=[
            pltpu.VMEM((count, block, block), BF16),
            pltpu.VMEM((n, node_dev, width), BF16),
            pltpu.VMEM((node_dev, hidden), F32),
            dma(()),
            *line_sems,
        ],
        compiler_params=params(collective_id=1, has_side_effects=True),
    )(
        col_block,
        first,
        ordered,
        w_first,
        b_first.reshape(1, -1),
        w_second,
        b_second.reshape(1, -1),
    )


def solution(mesh):
    groups, wide = mesh.shape["groups"], mesh.shape["wide"]
    side = 2 if groups < 4 and wide % 4 == 0 else 1
    depth = wide // (2 * side)
    placed = (
        P(("groups", "wide"), None),
        P(("groups", "wide")),
        P(("groups", "wide"), None, None),
        P(("groups", "wide")),
        P(("groups", "wide")),
        P(),
        P(),
        P(),
        P(),
    )
    return jax.shard_map(
        functools.partial(body, depth, side),
        mesh=mesh,
        in_specs=placed,
        out_specs=P(("groups", "wide"), None),
        check_vma=False,
    )
```

time: 263 us -> 103 us (0.39)
  waiting for transfers between devices: 133 us -> 0 us
  Pallas kernels: 0 us -> 98.8 us
  local copies, waits for them, and re-layouts: 74.5 us -> 3.65 us
  blocking collectives: 23.6 us -> 0 us
  between operations: 13.3 us -> 0.04 us
  matrix products: 12.4 us -> 0 us
  other arithmetic: 5.39 us -> 0.02 us
    all_gather x3 -> x0, waiting for transfers between devices: 133 us -> none  [the longest x2 101 us: aggregate(): piece = lax.all_gather(panel, 'wide', axis=0, tiled=True)]
    pallas_call x0 -> x3, Pallas kernels: none -> 98.8 us  [the longest x1 40.6 us: body(): pl.pallas_call(functools.partial(rows_kernel, depth, side), out_shape=(ja...]
    scatter x1 -> x0, local copies, waits for them, and re-layouts: 41.4 us -> none  [body(): jnp.zeros((node_dev + 1, feature_width), jnp.bfloat16).at[local]]
    gather x6 -> x0, local copies, waits for them, and re-layouts: 28 us -> none  [the longest x2 14.3 us: body(): jnp.take_along_axis(grid_values, order[:, :, :, None, None], axis=1)]
    all_gather x1 -> x0, blocking collectives: 23.6 us -> none  [body(): all_dest = lax.all_gather(dest, 'wide', axis=0, tiled=True)]
    dot_general x6 -> x0, matrix products: 12.4 us -> none  [the longest x4 10.2 us: aggregate(): jnp.einsum('gruij,gujw->riw', values, picked, preferred_element_type=jnp....]
    sort x1 -> x0, other arithmetic: 5.26 us -> none  [body(): order = jnp.argsort(grid_rows, axis=1, stable=True)]
  transfers between devices with their start and end apart: 3 -> 0, of which waited for: 3 -> 0; matrix products, arithmetic and copies ran while one was open for 8% -> 0% of each run, Pallas kernels for 0% -> 0%
where the time goes in v1:
time: 103 us; the launch traced here: 102 us
  Pallas kernels  98.8 us (96%)
  local copies, waits for them, and re-layouts  3.65 us (4%)
    pallas_call x1, Pallas kernels, body(): pl.pallas_call(functools.partial(rows_kernel, depth, side), out_shape=(ja...  40.6 us
    pallas_call x1, Pallas kernels, body(): pl.pallas_call(functools.partial(second_kernel, depth, side), out_shape=j...  38.3 us
    pallas_call x1, Pallas kernels, body(): pl.pallas_call(functools.partial(first_kernel, n), out_shape=(jax.ShapeDt...  19.9 us

profile of v1, /device:TPU:0, one launch (start us, length us, event | category | flops | bytes accessed | tf_op | source)
XLA Modules:
  0.0 102.5 jit_solution(13263454634362120250)
XLA Ops:
  0.0 0.8 eq.15
  0.8 0.1 copy.10
  1.0 0.1 copy.11
  1.1 0.7 reshape.53.order_ref
  1.8 40.6 %shard_map.91 = (f32[16384,128]{1,0:T(8,128)}, s32[128,128]{1,0:T(8,128)}) custom-call(s32[8,128]{1,0:T(8,128)} %bitcast.3, bf16[1024,128]{1,0:T(8,128)(2,1)} %loader_ref.1), custom_call_target="tpu_custom_call" | custom-call | tf_op jit(solution)/shard_map/pallas_call | solution.py:348
  42.4 19.9 %shard_map.92 = (bf16[1024,128]{1,0:T(8,128)(2,1)}, bf16[256,128,128]{2,1,0:T(8,128)(2,1)}) custom-call(s32[256]{0:T(256)} %col_ref.3, s32[256]{0:T(256)} %reshape.53.order_ref, s32[128,128]{1,0:T(8,128)} %get-tuple-element.9.inverse_ref, f32[16384,128]{1,0:T(8,128)} %get-tuple-element.10.table_ref, bf16[256,128,128]{2,1,0:T(8,128)(2,1)} %values_ref.1), custom_call_target="tpu_custom_call" | custom-call | tf_op jit(solution)/shard_map/pallas_call | solution.py:366
  62.3 38.3 %shard_map.93 = bf16[1024,256]{1,0:T(8,128)(2,1)} custom-call(s32[256]{0:T(256)} %col_ref.3, bf16[1024,128]{1,0:T(8,128)(2,1)} %get-tuple-element.11.first_ref, bf16[256,128,128]{2,1,0:T(8,128)(2,1)} %get-tuple-element.12.values_ref, bf16[128,256]{1,0:T(8,128)(2,1)} %w_first_ref.1, f32[1,256]{1,0:T(1,128)} %bitcast.4, bf16[256,256]{1,0:T(8,128)(2,1)} %w_second_ref.1, ...), custom_call_target="tpu_custom_call" | custom-call | tf_op jit(solution)/shard_map/pallas_call | solution.py:382
  100.6 1.9 %copy.13 = bf16[1024,256]{1,0:T(8,128)(2,1)} copy(bf16[1024,256]{1,0:T(8,128)(2,1)} %shard_map.93) | data formatting | bytes 1048576
  (2 shorter events, 0.0 us)

commit v2 on v1

--- a/solution.py
+++ b/solution.py
@@ -147,8 +147,8 @@
 
 
 def rows_kernel(
-    depth, side, dest_ref, loader_ref, table, inverse_int,
-    rows_buf, dest_buf, inverse, dest_send, dest_recv, *sems
+    depth, side, dest_ref, loader_ref, table_ref, inverse_int,
+    rows_buf, dest_buf, table, inverse, table_sem, dest_send, dest_recv, *sems
 ):
     n = depth * side * 2
     node_dev = loader_ref.shape[0]
@@ -212,9 +212,14 @@
 
         lax.fori_loop(0, 2, one, 0)
 
+    def table_copy(slot):
+        part = pl.ds(pl.multiple_of(slot * node_dev, node_dev), node_dev)
+        return pltpu.make_async_copy(table.at[part], table_ref.at[part], table_sem.at[slot])
+
     def widen(slot):
         start = pl.multiple_of(slot * node_dev, node_dev)
         table[pl.ds(start, node_dev), :] = rows_buf[slot].astype(F32)
+        table_copy(slot).start()
 
     gather(depth, side, rows_buf, loader_ref, sems, invert_two, widen)
 
@@ -223,6 +228,12 @@
         return _
 
     lax.fori_loop(1, n, drain_dest, 0)
+
+    def drain_table(slot, _):
+        table_copy(slot).wait()
+        return _
+
+    lax.fori_loop(0, n, drain_table, 0)
 
     inverse_int[...] = (
         inverse[:blocks, :] * float(block) + inverse[blocks:, :]
@@ -241,8 +252,11 @@
 
 def first_kernel(
     n, col_ref, order_ref, inverse_ref, table_ref, values_ref, first_ref, ordered_ref,
-    values, picked, total, local_sem
+    values, table, picked, total, local_sem
 ):
+    load = pltpu.make_async_copy(table_ref, table, local_sem.at[2])
+    load.start()
+
     def load_block(at, _):
         pltpu.make_async_copy(
             values_ref.at[order_ref[at]], values.at[at], local_sem.at[0]
@@ -258,13 +272,15 @@
         column = col_ref[(t // 2) * slots + t % 2]
 
         def fetch(j, _):
-            for k in range(16):
-                row = inverse_ref[column, j * 16 + k]
-                picked[pl.ds(t * block + j * 16 + k, 1), :] = table_ref[pl.ds(row, 1), :]
+            rows = [inverse_ref[column, j * 32 + k] for k in range(32)]
+            rows = [table[pl.ds(row, 1), :] for row in rows]
+            for k, row in enumerate(rows):
+                picked[pl.ds(t * block + j * 32 + k, 1), :] = row
             return _
 
-        return lax.fori_loop(0, block // 16, fetch, _)
-
+        return lax.fori_loop(0, block // 32, fetch, _)
+
+    load.wait()
     lax.fori_loop(0, 2 * n, pick, 0)
     pltpu.make_async_copy(values_ref, values, local_sem.at[0]).wait()
     store = pltpu.make_async_copy(values, ordered_ref, local_sem.at[1])
@@ -352,11 +368,13 @@
             jax.ShapeDtypeStruct((blocks, block), I32),
         ),
         in_specs=[vmem] * 2,
-        out_specs=(vmem, vmem),
+        out_specs=(anywhere, vmem),
         scratch_shapes=[
             pltpu.VMEM((n, node_dev, width), BF16),
             pltpu.VMEM((n, row_blocks, block), I32),
+            pltpu.VMEM((n * node_dev, width), F32),
             pltpu.VMEM((2 * blocks, block), F32),
+            dma((n,)),
             dma((n,)),
             dma((n,)),
             *line_sems,
@@ -369,13 +387,14 @@
             jax.ShapeDtypeStruct((node_dev, width), BF16),
             jax.ShapeDtypeStruct(block_values.shape, BF16),
         ),
-        in_specs=[smem, smem, smem, vmem, anywhere],
+        in_specs=[smem, smem, smem, anywhere, anywhere],
         out_specs=(vmem, anywhere),
         scratch_shapes=[
             pltpu.VMEM((count, block, block), BF16),
+            pltpu.VMEM((n * node_dev, width), F32),
             pltpu.VMEM((n * used * block, width), F32),
             pltpu.VMEM((node_dev, width), F32),
-            dma((2,)),
+            dma((3,)),
         ],
         compiler_params=params(),
     )(col_block, order, inverse, table, block_values)

time: 103 us -> 101 us (0.981)
  Pallas kernels: 98.8 us -> 97 us
    pallas_call x1, Pallas kernels: 40.6 us -> 38.3 us  [body(): pl.pallas_call(functools.partial(rows_kernel, depth, side), out_shape=(ja...]
where the time goes in v2:
time: 101 us
  Pallas kernels  97 us (96%)
  local copies, waits for them, and re-layouts  3.65 us (4%)
    pallas_call x1, Pallas kernels, body(): pl.pallas_call(functools.partial(second_kernel, depth, side), out_shape=j...  38.4 us
    pallas_call x1, Pallas kernels, body(): pl.pallas_call(functools.partial(rows_kernel, depth, side), out_shape=(ja...  38.3 us
    pallas_call x1, Pallas kernels, body(): pl.pallas_call(functools.partial(first_kernel, n), out_shape=(jax.ShapeDt...  20.2 us

profile of v2, /device:TPU:0, one launch (start us, length us, event | category | flops | bytes accessed | tf_op | source)
XLA Modules:
  0.0 100.7 jit_solution(11715150106306462538)
XLA Ops:
  0.0 0.8 eq.15
  0.8 0.1 copy.10
  1.0 0.1 copy.11
  1.1 0.7 reshape.53.order_ref
  1.8 38.3 %shard_map.91 = (f32[16384,128]{1,0:T(8,128)}, s32[128,128]{1,0:T(8,128)}) custom-call(s32[8,128]{1,0:T(8,128)} %bitcast.3, bf16[1024,128]{1,0:T(8,128)(2,1)} %loader_ref.1), custom_call_target="tpu_custom_call" | custom-call | tf_op jit(solution)/shard_map/pallas_call | solution.py:364
  40.1 20.2 %shard_map.92 = (bf16[1024,128]{1,0:T(8,128)(2,1)}, bf16[256,128,128]{2,1,0:T(8,128)(2,1)}) custom-call(s32[256]{0:T(256)} %col_ref.3, s32[256]{0:T(256)} %reshape.53.order_ref, s32[128,128]{1,0:T(8,128)} %get-tuple-element.9.inverse_ref, f32[16384,128]{1,0:T(8,128)} %get-tuple-element.10.table_ref, bf16[256,128,128]{2,1,0:T(8,128)(2,1)} %values_ref.1), custom_call_target="tpu_custom_call" | custom-call | tf_op jit(solution)/shard_map/pallas_call | solution.py:384
  60.4 38.4 %shard_map.93 = bf16[1024,256]{1,0:T(8,128)(2,1)} custom-call(s32[256]{0:T(256)} %col_ref.3, bf16[1024,128]{1,0:T(8,128)(2,1)} %get-tuple-element.11.first_ref, bf16[256,128,128]{2,1,0:T(8,128)(2,1)} %get-tuple-element.12.values_ref, bf16[128,256]{1,0:T(8,128)(2,1)} %w_first_ref.1, f32[1,256]{1,0:T(1,128)} %bitcast.4, bf16[256,256]{1,0:T(8,128)(2,1)} %w_second_ref.1, ...), custom_call_target="tpu_custom_call" | custom-call | tf_op jit(solution)/shard_map/pallas_call | solution.py:401
  98.8 1.9 %copy.13 = bf16[1024,256]{1,0:T(8,128)(2,1)} copy(bf16[1024,256]{1,0:T(8,128)(2,1)} %shard_map.93) | data formatting | bytes 1048576
  (2 shorter events, 0.0 us)

commit v3 on v2

--- a/solution.py
+++ b/solution.py
@@ -38,18 +38,22 @@
     def slot_of(at_z, at_y, at_core):
         return (at_z * side + at_y) * 2 + at_core
 
-    def copy(source_ref, slot, send, target):
+    rows = buf.shape[1]
+    cut = rows * 3 // 4
+    parts = (pl.ds(0, cut), pl.ds(cut, rows - cut))
+
+    def copy(slot, part, send, target):
         return pltpu.make_async_remote_copy(
-            src_ref=source_ref,
-            dst_ref=buf.at[slot],
+            src_ref=buf.at[slot, parts[part]],
+            dst_ref=buf.at[slot, parts[part]],
             send_sem=send,
-            recv_sem=recv.at[slot],
+            recv_sem=recv.at[part, slot],
             device_id={"wide": target},
             device_id_type=MESH,
         )
 
-    def arrived(slot):
-        copy(buf.at[slot], slot, pair_send.at[0, 0], pair).wait_recv()
+    def arrived(slot, part):
+        copy(slot, part, pair_send.at[0, 0], pair).wait_recv()
 
     def place(d):
         off = (d + 1) // 2
@@ -63,12 +67,17 @@
     steps = 2 * depth - 1
     buf[me] = own_ref[...]
 
-    def line_copies(d, slot):
-        source = buf.at[slot]
+    kinds = (1, 0, 2) if side == 2 else (1, 0)
+
+    def kind_of(q, at_z):
+        at_y = 1 - lane_y if q == 2 else lane_y
+        return slot_of(at_z, at_y, core), min(q, 1)
+
+    def line_copies(d, q, slot, part):
         return (
-            (copy(source, slot, line_send.at[0, d], right),
+            (copy(slot, part, line_send.at[0, q, d], right),
              ((d == 0) | (d % 2 == 1)) & (lane_z < depth - 1)),
-            (copy(source, slot, line_send.at[1, d], left),
+            (copy(slot, part, line_send.at[1, q, d], left),
              (d % 2 == 0) & (lane_z > 0)),
         )
 
@@ -77,17 +86,21 @@
 
         @pl.when(valid & (d < steps))
         def _line():
-            slot = slot_of(at_z, lane_y, core)
-
-            @pl.when(d > 0)
-            def _wait():
-                arrived(slot)
-
-            for one, go in line_copies(d, slot):
-                pl.when(go)(one.start)
-            if side == 2:
-                copy(buf.at[slot], slot, side_send.at[d], across).start()
-            copy(buf.at[slot], slot, pair_send.at[0, d], pair).start()
+            for q in kinds:
+                slot, part = kind_of(q, at_z)
+                if q == 2:
+                    arrived(slot, part)
+                else:
+                    pl.when(d > 0)(functools.partial(arrived, slot, part))
+                if side == 2 and q == 1:
+                    pl.when(d == 0)(
+                        copy(slot, part, side_send.at[steps], across).start
+                    )
+                for one, go in line_copies(d, q, slot, part):
+                    pl.when(go)(one.start)
+                if side == 2 and q == 0:
+                    copy(slot, part, side_send.at[d], across).start()
+                copy(slot, part, pair_send.at[q, d], pair).start()
 
         extra(d)
 
@@ -97,8 +110,8 @@
             @pl.when(back_valid & (d - 2 < steps))
             def _side():
                 slot = slot_of(back_z, 1 - lane_y, core)
-                arrived(slot)
-                copy(buf.at[slot], slot, pair_send.at[1, d - 2], pair).start()
+                arrived(slot, 0)
+                copy(slot, 0, pair_send.at[3, d - 2], pair).start()
 
         def kind(k, _):
             lag = jnp.where(k == 0, 0, jnp.where(k == 3, 4, 2))
@@ -113,7 +126,8 @@
             def _process():
                 @pl.when(from_pair == 1)
                 def _wait():
-                    arrived(slot)
+                    arrived(slot, 0)
+                    arrived(slot, 1)
 
                 process(slot)
 
@@ -132,14 +146,20 @@
 
         @pl.when(valid)
         def _drain():
-            slot = slot_of(at_z, lane_y, core)
-            for one, go in line_copies(d, slot):
-                pl.when(go)(one.wait_send)
+            for q in kinds:
+                slot, part = kind_of(q, at_z)
+                for one, go in line_copies(d, q, slot, part):
+                    pl.when(go)(one.wait_send)
+                copy(slot, part, pair_send.at[q, d], pair).wait_send()
+                if side == 2 and q == 1:
+                    pl.when(d == 0)(
+                        copy(slot, part, side_send.at[steps], across).wait_send
+                    )
+                if side == 2 and q == 0:
+                    copy(slot, part, side_send.at[d], across).wait_send()
             if side == 2:
-                copy(buf.at[slot], slot, side_send.at[d], across).wait_send()
                 other = slot_of(at_z, 1 - lane_y, core)
-                copy(buf.at[other], other, pair_send.at[1, d], pair).wait_send()
-            copy(buf.at[slot], slot, pair_send.at[0, d], pair).wait_send()
+                copy(other, 0, pair_send.at[3, d], pair).wait_send()
 
         return _
 
@@ -356,7 +376,7 @@
     smem = pl.BlockSpec(memory_space=pltpu.SMEM)
     dma = pltpu.SemaphoreType.DMA
     anywhere = pl.BlockSpec(memory_space=pl.ANY)
-    line_sems = [dma((2, steps)), dma((steps,)), dma((2, steps)), dma((n,))]
+    line_sems = [dma((2, 3, steps)), dma((steps + 1,)), dma((4, steps)), dma((2, n))]
 
     def params(**more):
         return pltpu.CompilerParams(vmem_limit_bytes=60 * 1024 * 1024, **more)

time: 101 us -> 105 us (1.040)
  Pallas kernels: 97 us -> 101 us
    pallas_call x1, Pallas kernels: 38.3 us -> 40.4 us  [body(): pl.pallas_call(functools.partial(rows_kernel, depth, side), out_shape=(ja...]
    pallas_call x1, Pallas kernels: 38.4 us -> 40.1 us  [body(): pl.pallas_call(functools.partial(second_kernel, depth, side), out_shape=j...]
where the time goes in v3:
time: 105 us
  Pallas kernels  101 us (96%)
  local copies, waits for them, and re-layouts  3.65 us (3%)
    pallas_call x1, Pallas kernels, body(): pl.pallas_call(functools.partial(rows_kernel, depth, side), out_shape=(ja...  40.4 us
    pallas_call x1, Pallas kernels, body(): pl.pallas_call(functools.partial(second_kernel, depth, side), out_shape=j...  40.1 us
    pallas_call x1, Pallas kernels, body(): pl.pallas_call(functools.partial(first_kernel, n), out_shape=(jax.ShapeDt...  20.2 us

profile of v3, /device:TPU:0, one launch (start us, length us, event | category | flops | bytes accessed | tf_op | source)
XLA Modules:
  0.0 104.5 jit_solution(16095610201558918694)
XLA Ops:
  0.0 0.8 eq.15
  0.8 0.1 copy.10
  1.0 0.1 copy.11
  1.1 0.7 reshape.53.order_ref
  1.8 40.4 %shard_map.91 = (f32[16384,128]{1,0:T(8,128)}, s32[128,128]{1,0:T(8,128)}) custom-call(s32[8,128]{1,0:T(8,128)} %bitcast.3, bf16[1024,128]{1,0:T(8,128)(2,1)} %loader_ref.1), custom_call_target="tpu_custom_call" | custom-call | tf_op jit(solution)/shard_map/pallas_call | solution.py:384
  42.3 20.2 %shard_map.92 = (bf16[1024,128]{1,0:T(8,128)(2,1)}, bf16[256,128,128]{2,1,0:T(8,128)(2,1)}) custom-call(s32[256]{0:T(256)} %col_ref.3, s32[256]{0:T(256)} %reshape.53.order_ref, s32[128,128]{1,0:T(8,128)} %get-tuple-element.9.inverse_ref, f32[16384,128]{1,0:T(8,128)} %get-tuple-element.10.table_ref, bf16[256,128,128]{2,1,0:T(8,128)(2,1)} %values_ref.1), custom_call_target="tpu_custom_call" | custom-call | tf_op jit(solution)/shard_map/pallas_call | solution.py:404
  62.5 40.1 %shard_map.93 = bf16[1024,256]{1,0:T(8,128)(2,1)} custom-call(s32[256]{0:T(256)} %col_ref.3, bf16[1024,128]{1,0:T(8,128)(2,1)} %get-tuple-element.11.first_ref, bf16[256,128,128]{2,1,0:T(8,128)(2,1)} %get-tuple-element.12.values_ref, bf16[128,256]{1,0:T(8,128)(2,1)} %w_first_ref.1, f32[1,256]{1,0:T(1,128)} %bitcast.4, bf16[256,256]{1,0:T(8,128)(2,1)} %w_second_ref.1, ...), custom_call_target="tpu_custom_call" | custom-call | tf_op jit(solution)/shard_map/pallas_call | solution.py:421
  102.6 1.9 %copy.13 = bf16[1024,256]{1,0:T(8,128)(2,1)} copy(bf16[1024,256]{1,0:T(8,128)(2,1)} %shard_map.93) | data formatting | bytes 1048576
  (2 shorter events, 0.0 us)
